TPU v7x, 32 devices: a whole 2x2x4 slice. The times are simulated.
32 devices in a mesh: section: 4 (over y, x), seq: 4 (over z), tensor: 2 (over core).
Axes of the slice: x: 2, y: 2, z: 4, core: 2. Of those that a mesh axis runs over, the one named last changes fastest.
Arguments:
- values: bfloat16 [1024, 8192], P('seq', ('section', 'tensor')), may hold values from -6 to 6
- gate_in: bfloat16 [1024, 8192], P('seq', ('section', 'tensor')), may hold values from -6 to 6
- b_proj: bfloat16 [1024, 4, 128], P('seq', 'section'), may hold values from -0.5 to 0.5
- c_proj: bfloat16 [1024, 4, 128], P('seq', 'section'), may hold values from -0.5 to 0.5
- step_size: float32 [128, 1024], P(('section', 'tensor'), 'seq'), may hold values from 0.25 to 2
- decay_rate: float32 [128], P(('section', 'tensor')), may hold values from 0.0009765625 to 0.1
- norm_gain: float32 [8192], P(('section', 'tensor')), may hold values from 0.5 to 1.5
- cotangent: bfloat16 [1024, 8192], P('seq', ('section', 'tensor')), may hold values from -6 to 6
Outputs:
- result: bfloat16 [1024, 8192], P('seq', ('section', 'tensor'))
- grad_values: bfloat16 [1024, 8192], P('seq', ('section', 'tensor'))
- grad_gate: bfloat16 [1024, 8192], P('seq', ('section', 'tensor'))
- grad_b: float32 [1024, 4, 128], P('seq', 'section')
- grad_c: float32 [1024, 4, 128], P('seq', 'section')
- grad_step: float32 [128, 1024], P(('section', 'tensor'), 'seq')
- grad_rate: float32 [128], P(('section', 'tensor'))
- grad_gain: float32 [8192], P(('section', 'tensor'))
All inputs are finite; a program needn't handle non-finite values.
Results may differ from a plain program's by a relative error of at most 0.001.
Values sent between devices are 32-bit elements; how exact they have to be, the bound alone decides.
A program may use at most 128 MiB of HBM per device.

v0:
```python
import jax
import jax.numpy as jnp
from jax import lax
from jax.sharding import PartitionSpec as P

P_SIZE = 64
N = 128
BLOCK = 128


HIGHEST = lax.Precision.HIGHEST
EPSILON = 1e-05
CLIP = 90.0


def carried_in(value, axis, join, neutral, backward):
    count, mine = (lax.axis_size(axis), lax.axis_index(axis))
    pieces = jax.tree.map(lambda part: lax.all_gather(part, axis), value)
    if backward:
        pieces = jax.tree.map(lambda part: part[::-1], pieces)
        mine = count - 1 - mine
    total = jax.tree.map(
        lambda part, zero: jnp.full_like(part, 0) + jnp.asarray(zero, part.dtype), value, neutral
    )

    def hop(position, total):
        longer = join(total, jax.tree.map(lambda part: part[position], pieces))
        return jax.tree.map(lambda new, old: jnp.where(position < mine, new, old), longer, total)

    return lax.fori_loop(0, count - 1, hop, total)


def block_scan(inputs_h, b_rows, c_rows, steps_dt, rates, state_in):
    length = inputs_h.shape[0]
    heads = inputs_h.shape[1]
    blocks = length // BLOCK
    value_blocks = inputs_h.reshape(blocks, BLOCK, heads, P_SIZE)
    b_blocks = b_rows.reshape(blocks, BLOCK, N)
    c_blocks = c_rows.reshape(blocks, BLOCK, N)
    dt_blocks = steps_dt.reshape(heads, blocks, BLOCK).transpose(1, 0, 2)
    position = jnp.arange(BLOCK)
    causal = (position[:, None] >= position[None, :])[None]

    def advance(state, item):
        value_blk, b_blk, c_blk, dt_blk = item
        cumulative = jnp.cumsum(-dt_blk * rates[:, None], axis=1)
        spread = cumulative[:, :, None] - cumulative[:, None, :]
        segment = jnp.where(causal, jnp.exp(jnp.where(causal, spread, 0.0)), 0.0)
        intersection_m = jnp.dot(
            c_blk, b_blk.T, precision=HIGHEST, preferred_element_type=jnp.float32
        )
        weights = intersection_m[None] * segment * dt_blk[:, None, :]
        inner = jnp.einsum("hij,jhp->ihp", weights, value_blk, precision=HIGHEST)
        carried = (
            jnp.einsum("in,hnp->ihp", c_blk, state, precision=HIGHEST)
            * jnp.exp(cumulative).T[:, :, None]
        )
        tail = jnp.exp(cumulative[:, -1:] - cumulative) * dt_blk
        fresh = jnp.exp(cumulative[:, -1])[:, None, None] * state + jnp.einsum(
            "hj,jn,jhp->hnp", tail, b_blk, value_blk, precision=HIGHEST
        )
        return (fresh, inner + carried)

    state_out, outputs = lax.scan(
        jax.checkpoint(advance), state_in, (value_blocks, b_blocks, c_blocks, dt_blocks)
    )
    return (outputs.reshape(length, heads, P_SIZE), state_out)


def link_states(earlier, later):
    return (earlier[0] * later[0], later[0][:, None, None] * earlier[1] + later[1])


def local(values, gate_in, b_proj, c_proj, step_size, decay_rate, norm_gain, cotangent):
    tokens_here, channels = values.shape
    heads = decay_rate.shape[0]
    values_f = values.astype(jnp.float32).reshape(tokens_here, heads, P_SIZE)
    gate_f = gate_in.astype(jnp.float32)
    b_rows = b_proj[:, 0, :].astype(jnp.float32)
    c_rows = c_proj[:, 0, :].astype(jnp.float32)
    cumulative = jnp.cumsum(-step_size * decay_rate[:, None], axis=1)
    log_total = cumulative[:, -1]
    tail = jnp.exp(log_total[:, None] - cumulative) * step_size
    local_end = jnp.einsum("hj,jn,jhp->hnp", tail, b_rows, values_f, precision=HIGHEST)
    decay_total = jnp.exp(log_total)
    empty_state = jnp.zeros_like(local_end)
    identity = (jnp.ones_like(decay_total), empty_state)
    state_in = carried_in((decay_total, local_end), "seq", link_states, identity, False)[1]
    (mixed, state_out), pullback = jax.vjp(
        block_scan, values_f, b_rows, c_rows, step_size, decay_rate, state_in
    )
    flat = mixed.reshape(tokens_here, channels)
    sigm = jax.nn.sigmoid(gate_f)
    swish = gate_f * sigm
    gated = flat * swish
    group_width = channels * lax.axis_size("tensor")
    squares_sum = lax.psum(jnp.sum(gated * gated, axis=1), "tensor")
    scale = lax.rsqrt(squares_sum / group_width + EPSILON)
    normed = gated * scale[:, None]
    result = (normed * norm_gain).astype(jnp.bfloat16)
    upstream = cotangent.astype(jnp.float32)
    weighted = upstream * norm_gain
    inner_sum = lax.psum(jnp.sum(weighted * gated, axis=1), "tensor")
    d_gated = (
        scale[:, None] * weighted
        - gated * (scale * scale * scale * inner_sum / group_width)[:, None]
    )
    gain_part = jnp.sum(upstream * normed, axis=0)
    d_mixed = (d_gated * swish).reshape(tokens_here, heads, P_SIZE)
    d_gate = d_gated * flat * sigm * (1.0 + gate_f * (1.0 - sigm))
    partial_grads = pullback((d_mixed, empty_state))
    state_grad = carried_in((decay_total, partial_grads[5]), "seq", link_states, identity, True)[1]
    full_grads = pullback((d_mixed, state_grad))
    b_grad, c_grad = lax.psum((full_grads[1], full_grads[2]), "tensor")
    rate_grad, gain_grad = lax.psum((full_grads[4], gain_part), "seq")
    total = lax.psum(
        jnp.sum(rate_grad * rate_grad) + jnp.sum(gain_grad * gain_grad), ("section", "tensor")
    )
    factor = CLIP / jnp.maximum(jnp.sqrt(total), CLIP)
    grad_values = full_grads[0].reshape(tokens_here, channels).astype(jnp.bfloat16)
    return (
        result,
        grad_values,
        d_gate.astype(jnp.bfloat16),
        b_grad[:, None, :],
        c_grad[:, None, :],
        full_grads[3],
        rate_grad * factor,
        gain_grad * factor,
    )


def solution(mesh):
    return jax.shard_map(
        local,
        mesh=mesh,
        in_specs=(
            P("seq", ("section", "tensor")),
            P("seq", ("section", "tensor")),
            P("seq", "section", None),
            P("seq", "section", None),
            P(("section", "tensor"), "seq"),
            P(("section", "tensor")),
            P(("section", "tensor")),
            P("seq", ("section", "tensor")),
        ),
        out_specs=(
            P("seq", ("section", "tensor")),
            P("seq", ("section", "tensor")),
            P("seq", ("section", "tensor")),
            P("seq", "section", None),
            P("seq", "section", None),
            P(("section", "tensor"), "seq"),
            P(("section", "tensor")),
            P(("section", "tensor")),
        ),
        check_vma=False,
    )
```

profile of v0, /device:TPU:0, one launch (start us, length us, event | category | flops | bytes accessed | tf_op | source)
XLA Modules:
  0.0 323.2 jit_solution(14279821024316011674)
XLA Ops:
  11.3 2.3 convolution_bitcast_fusion.7
  15.8 13.6 %all-reduce.2 = f32[64]{0:T(128)S(1)} all-reduce(f32[64]{0:T(128)S(1)} %dynamic-update-slice), channel_id=2, replica_groups=mesh['section'=4,'seq'=4,'tensor'=2] {'seq'}, use_global_device_ids=true, to_apply=%add.2 | all-reduce | flops 64 | bytes 512
  33.3 29.2 %all-gather.6.cloned.1.call-done = f32[64,128,64]{1,2,0:T(8,128)} async-done(((f32[16,128,64]{1,2,0:T(8,128)}), f32[64,128,64]{1,2,0:T(8,128)}) %all-gather.6.cloned.1.call-update) | async-done | bytes 2097168 | tf_op jit(solution)/shard_map/all_gather | solution.py:18
  62.5 12.3 %while.87 = (s32[]{:T(128)}, f32[16,128,64]{2,1,0:T(8,128)}, s32[]{:T(128)}, f32[4,16]{1,0:T(4,128)}, f32[4,16,128,64]{2,3,1,0:T(8,128)}, /*index=5*/s32[]{:T(128)}, s32[]{:T(128)}) while((s32[]{:T(128)}, f32[16,128,64]{2,1,0:T(8,128)}, s32[]{:T(128)}, f32[4,16]{1,0:T(4,128)}, f32[4,16,128,64]{2,3,1,0:T(8,128)}, ...), condition=%wide.region_3.4_spmd.clone, body=%wide.region_2.3_spmd.clone.sunk | while | flops 524292 | bytes 3670313 | solution.py:30
  67.9 2.4 fusion.168
  72.5 2.4 fusion.168
  76.4 38.2 %while.86 = (s32[]{:T(128)}, f32[16,128,64]{1,2,0:T(8,128)S(1)}, f32[2,128,16,64]{1,0,3,2:T(2,128)}, f32[2,16,128,64]{2,3,1,0:T(8,128)}, f32[2,16,128]{2,1,0:T(8...) while((s32[]{:T(128)}, f32[16,128,64]{1,2,0:T(8,128)S(1)}, ...), condition=%wide.region_6.7_spmd.clone.clone, body=%wide.region_4.6_spmd.clone.clone.sunk | while | flops 631379968 | bytes 6819345 | solution.py:64
  78.6 2.2 fusion.167
  80.8 13.1 %dynamic_update_slice.72 = f32[2,128,16,64]{1,0,3,2:T(2,128)} dynamic-update-slice(f32[2,128,16,64]{1,0,3,2:T(2,128)} %get-tuple-element.1508, f32[1,128,16,64]{1,0,3,2:T(1,128)S(1)} %bitcast.350, s32[]{:T(128)} %get-tuple-element.1506, s32[]{:T(128)} %constant.201.clone.1..sunk, s32[]{:T(128)} %constant.201.clone.1..sunk, s32[]{:T(128)} %constant.201.clone.1..sunk) | dynamic-update-slice | bytes 1048580 | tf_op jit(solution)/shard_map/jvp()/while/body/jit(dynamic_update_index_in_dim)/dynamic_update_slice | solution.py:64
  97.7 2.2 fusion.167
  99.9 13.1 %dynamic_update_slice.72 = f32[2,128,16,64]{1,0,3,2:T(2,128)} dynamic-update-slice(f32[2,128,16,64]{1,0,3,2:T(2,128)} %get-tuple-element.1508, f32[1,128,16,64]{1,0,3,2:T(1,128)S(1)} %bitcast.350, s32[]{:T(128)} %get-tuple-element.1506, s32[]{:T(128)} %constant.201.clone.1..sunk, s32[]{:T(128)} %constant.201.clone.1..sunk, s32[]{:T(128)} %constant.201.clone.1..sunk) | dynamic-update-slice | bytes 1048580 | tf_op jit(solution)/shard_map/jvp()/while/body/jit(dynamic_update_index_in_dim)/dynamic_update_slice | solution.py:64
  116.5 2.5 psum.49
  119.0 2.2 fusion.88
  121.1 2.4 psum.50
  123.6 3.4 %fusion.94 = (bf16[256,1024]{0,1:T(8,128)(2,1)}, f32[256,1024]{0,1:T(8,128)}, bf16[256,1024]{0,1:T(8,128)(2,1)}) fusion(bf16[256,1024]{0,1:T(8,128)(2,1)S(1)} %copy-done.1, f32[128,8,2,128]{3,2,1,0:T(2,128)} %bitcast.353, f32[256,1024]{0,1:T(8,128)S(1)} %get-tuple-element.1144, bf16[256,1024]{0,1:T(8,128)(2,1)} %copy.64, f32[256]{0:T(256)S(1)} %fusion.101, ...), kind=kLoop, calls=%fused_computation.150 | loop fusion | flops 5505024 | bytes 5249024 | tf_op jit(solution)/shard_map/convert_element_type | solution.py:124
  130.0 6.0 %while.88 = (s32[]{:T(128)}, f32[16,128,64]{1,2,0:T(8,128)S(1)}, f32[2,128,128]{2,1,0:T(8,128)S(1)}, f32[2,16,128]{2,1,0:T(8,128)S(1)}, f32[2,128,16,64]{1,3,2,0...) while((s32[]{:T(128)}, f32[16,128,64]{1,2,0:T(8,128)S(1)}, ...), condition=%wide.region_13.14_spmd.clone, body=%wide.region_11.13_spmd.clone.sunk | while | flops 202115072 | bytes 3940739 | solution.py:64
  138.1 43.7 %all-gather.8.cloned.1.call-done = f32[64,128,64]{1,2,0:T(8,128)} async-done(((f32[16,128,64]{1,2,0:T(8,128)}), f32[64,128,64]{1,2,0:T(8,128)}) %all-gather.8.cloned.1.call-update) | async-done | bytes 2097168 | tf_op jit(solution)/shard_map/all_gather | solution.py:18
  181.8 3.8 %copy.67 = f32[4,16,128,64]{3,2,1,0:T(8,128)} copy(f32[4,16,128,64]{2,3,1,0:T(8,128)} %bitcast.356) | data formatting | bytes 4194304 | tf_op jit(solution)/shard_map/all_gather | solution.py:18
  185.6 4.7 %rev.7 = f32[4,16,128,64]{3,2,1,0:T(8,128)} reverse(f32[4,16,128,64]{3,2,1,0:T(8,128)} %copy.67), dimensions={0} | reverse | bytes 4194304 | tf_op jit(solution)/shard_map/rev | solution.py:20
  190.2 4.5 %while.89 = (s32[]{:T(128)}, f32[16,128,64]{2,1,0:T(8,128)S(1)}, s32[]{:T(128)}, f32[4,16]{1,0:T(4,128)S(1)}, f32[4,16,128,64]{3,2,1,0:T(8,128)}, /*index=5*/s32[]{:T(128)}, s32[]{:T(128)}) while((s32[]{:T(128)}, f32[16,128,64]{2,1,0:T(8,128)S(1)}, s32[]{:T(128)}, f32[4,16]{1,0:T(4,128)S(1)}, f32[4,16,128,64]{3,2,1,0:T(8,128)}, ...), condition=%wide.region_15.16_spmd.clone, body=%wide.region_14.15_spmd.clone.sunk | while | flops 524292 | bytes 1573161 | solution.py:30
  197.9 71.6 %while.90 = (s32[]{:T(128)}, f32[16]{0:T(128)}, f32[16,128,64]{1,2,0:T(8,128)S(1)}, bf16[2,128,16,64]{1,3,2,0:T(8,128)(2,1)}, f32[2,128,128]{2,1,0:T(8,128)}, /*...) while((s32[]{:T(128)}, f32[16]{0:T(128)}, ...), condition=%wide.region_27.28_spmd.clone, body=%wide.region_16.27_spmd.clone.sunk | while | flops 1492328448 | bytes 15495879 | solution.py:64
  208.7 2.1 multiply_bitcast_fusion.6
  213.5 3.9 %fusion.192 = (f32[16,128]{1,0:T(8,128)S(1)}, f32[16,128]{1,0:T(8,128)S(1)}, f32[16,128]{1,0:T(8,128)}, f32[128,128]{1,0:T(8,128)}) fusion(f32[16,128]{1,0:T(8,128)S(1)} %reduce_window_sum.87, f32[16,128]{1,0:T(8,128)S(1)} %dynamic-slice_bitcast_fusion.30, f32[128,128]{1,0:T(8,128)S(1)} %fusion.191, pred[128,128]{1,0:T(8,128)(4,1)} %bitcast.359, ...), kind=kOutput, calls=%fused_computation.86.clone.1 | convolution fusion | flops 205236224 | bytes 1236992 | tf_op jit(solution)/shard_map/transpose(jvp())/while/body/eval_jaxpr/checkpoint/hij,jhp->ihp/dot_general | solution.py:53
  218.2 2.5 reduce_window_sum.88
  229.0 3.1 fusion.196
  244.5 2.1 multiply_bitcast_fusion.6
  249.4 3.9 %fusion.192 = (f32[16,128]{1,0:T(8,128)S(1)}, f32[16,128]{1,0:T(8,128)S(1)}, f32[16,128]{1,0:T(8,128)}, f32[128,128]{1,0:T(8,128)}) fusion(f32[16,128]{1,0:T(8,128)S(1)} %reduce_window_sum.87, f32[16,128]{1,0:T(8,128)S(1)} %dynamic-slice_bitcast_fusion.30, f32[128,128]{1,0:T(8,128)S(1)} %fusion.191, pred[128,128]{1,0:T(8,128)(4,1)} %bitcast.359, ...), kind=kOutput, calls=%fused_computation.86.clone.1 | convolution fusion | flops 205236224 | bytes 1236992 | tf_op jit(solution)/shard_map/transpose(jvp())/while/body/eval_jaxpr/checkpoint/hij,jhp->ihp/dot_general | solution.py:53
  254.0 2.5 reduce_window_sum.88
  264.8 3.1 fusion.196
  269.5 9.8 %all-reduce.3 = (f32[16]{0:T(128)S(1)}, f32[1024]{0:T(1024)S(1)}) all-reduce(f32[16]{0:T(128)} %get-tuple-element.762, f32[1024]{0:T(1024)} %get-tuple-element.1053), channel_id=1, replica_groups=mesh['section'=4,'seq'=4,'tensor'=2] {'seq'}, use_global_device_ids=true, to_apply=%region_30.31 | all-reduce | flops 1040 | bytes 8320 | tf_op jit(solution)/shard_map/psum | solution.py:115
  283.8 12.3 %psum.55 = f32[]{:T(128)} all-reduce(f32[]{:T(128)S(6)} %add.145), channel_id=1, replica_groups=mesh['section'=4,'seq'=4,'tensor'=2] {'section','tensor'}, use_global_device_ids=true, to_apply=%region_35.36 | all-reduce | flops 1 | bytes 8 | tf_op jit(solution)/shard_map/psum | solution.py:116
  302.0 11.5 %all-reduce.7.cloned.1.call-done = (f32[256,1,128]{2,1,0:T(1,128)}, f32[256,1,128]{2,1,0:T(1,128)}) async-done(((f32[256,1,128]{2,1,0:T(1,128)}, f32[256,1,128]{2,1,0:T(1,128)}), (f32[256,1,128]{2,1,0:T(1,128)}, f32[256,1,128]{2,1,0:T(1,128)})) %all-reduce.7.cloned.1.call-update) | async-done | bytes 262160 | tf_op jit(solution)/shard_map/psum | solution.py:114
  (232 shorter events, 106.0 us)
Async XLA Ops:
  7.2 7.1 %copy-start.23 = (u32[32]{0:T(128)S(1)}, u32[32]{0:T(128)}, u32[]{:S(2)}) copy-start(u32[32]{0:T(128)} %constant.218) | copy-start | bytes 388
  7.2 7.0 %copy-start.16 = (f32[16,256]{1,0:T(8,128)S(1)}, f32[16,256]{1,0:T(8,128)}, u32[]{:S(2)}) copy-start(f32[16,256]{1,0:T(8,128)} %param.22) | copy-start | bytes 49156
  7.2 55.3 %all-gather.6.cloned.1.call-start = ((), (), s32[]{:S(2)}) async-start(), calls=%async_computation | async-start | bytes 2621440 | tf_op jit(solution)/shard_map/all_gather | solution.py:18
  9.9 20.3 %copy-start.17 = (bf16[256,1,128]{2,0,1:T(8,128)(2,1)S(1)}, bf16[256,1,128]{2,0,1:T(8,128)(2,1)}, u32[]{:S(2)}) copy-start(bf16[256,1,128]{2,0,1:T(8,128)(2,1)} %param.21) | copy-start | bytes 196612
  9.9 20.3 %copy-start.12 = (bf16[256,1,128]{2,0,1:T(8,128)(2,1)S(1)}, bf16[256,1,128]{2,0,1:T(8,128)(2,1)}, u32[]{:S(2)}) copy-start(bf16[256,1,128]{2,0,1:T(8,128)(2,1)} %param.20) | copy-start | bytes 196612
  11.2 19.0 %copy-start.11 = (bf16[256,1024]{1,0:T(8,128)(2,1)S(1)}, bf16[256,1024]{1,0:T(8,128)(2,1)}, u32[]{:S(2)}) copy-start(bf16[256,1024]{1,0:T(8,128)(2,1)} %param.19) | copy-start | bytes 1572868
  13.6 168.2 %all-gather.8.cloned.1.call-start = ((), (), s32[]{:S(2)}) async-start(), calls=%async_computation.1 | async-start | bytes 2621440 | tf_op jit(solution)/shard_map/all_gather | solution.py:18
  76.4 42.6 %copy-start.21 = (f32[1024]{0:T(1024)S(1)}, f32[1024]{0:T(1024)}, u32[]{:S(2)}) copy-start(f32[1024]{0:T(1024)} %param.24) | copy-start | bytes 12292
  114.7 8.9 %copy-start.1 = (bf16[256,1024]{0,1:T(8,128)(2,1)S(1)}, bf16[256,1024]{0,1:T(8,128)(2,1)}, u32[]{:S(2)}) copy-start(bf16[256,1024]{0,1:T(8,128)(2,1)} %copy.63) | copy-start | bytes 1572868
  130.0 7.1 %copy-start.22 = (f32[4,16]{1,0:T(4,128)S(1)}, f32[4,16]{1,0:T(4,128)}, u32[]{:S(2)}) copy-start(f32[4,16]{1,0:T(4,128)} %get-tuple-element.1663) | copy-start | bytes 772
  130.0 7.1 %copy-start.3 = (bf16[256,1024]{0,1:T(8,128)(2,1)S(1)}, bf16[256,1024]{0,1:T(8,128)(2,1)}, u32[]{:S(2)}) copy-start(bf16[256,1024]{0,1:T(8,128)(2,1)} %get-tuple-element.1160) | copy-start | bytes 1572868
  136.8 176.7 %all-reduce.7.cloned.1.call-start = ((), (), s32[]{:S(2)}) async-start(), calls=%async_computation.2 | async-start | bytes 524288 | tf_op jit(solution)/shard_map/psum | solution.py:114
  212.0 5.4 %copy-start.2 = (f32[16,128]{1,0:T(8,128)S(1)}, f32[16,128]{1,0:T(8,128)}, u32[]{:S(2)}) copy-start(f32[16,128]{1,0:T(8,128)} %get-tuple-element.1464) | copy-start | bytes 24580 | tf_op jit(solution)/shard_map/transpose(jvp())/while
  212.1 5.4 %copy-start.9 = (f32[16,1]{1,0:T(8,128)S(1)}, f32[16,1]{1,0:T(8,128)}, u32[]{:S(2)}) copy-start(f32[16,1]{1,0:T(8,128)} %get-tuple-element.1466) | copy-start | bytes 196 | tf_op jit(solution)/shard_map/transpose(jvp())/while
  212.1 5.4 %copy-start.10 = (f32[16,1]{1,0:T(8,128)S(1)}, f32[16,1]{1,0:T(8,128)}, u32[]{:S(2)}) copy-start(f32[16,1]{1,0:T(8,128)} %copy.112) | copy-start | bytes 196 | tf_op jit(solution)/shard_map/transpose(jvp())/while
  212.1 5.4 %copy-start.14 = (f32[16]{0:T(128)S(1)}, f32[16]{0:T(128)}, u32[]{:S(2)}) copy-start(f32[16]{0:T(128)} %copy-done.13) | copy-start | bytes 196 | tf_op jit(solution)/shard_map/transpose(jvp())/while
  220.7 11.4 %copy-start.15 = (f32[16]{0:T(128)S(1)}, f32[16]{0:T(128)}, u32[]{:S(2)}) copy-start(f32[16]{0:T(128)} %copy-done.13) | copy-start | bytes 196 | tf_op jit(solution)/shard_map/transpose(jvp())/while
  220.7 11.5 %copy-start.4 = (f32[128,16]{0,1:T(8,128)S(1)}, f32[128,16]{0,1:T(8,128)}, u32[]{:S(2)}) copy-start(f32[128,16]{0,1:T(8,128)} %get-tuple-element.1467) | copy-start | bytes 24580 | tf_op jit(solution)/shard_map/transpose(jvp())/while
  220.7 12.3 %copy-start.5 = (f32[16,128]{1,0:T(8,128)S(1)}, f32[16,128]{1,0:T(8,128)}, u32[]{:S(2)}) copy-start(f32[16,128]{1,0:T(8,128)} %reduce_window_sum.88) | copy-start | bytes 24580 | tf_op jit(solution)/shard_map/transpose(jvp())/while
  223.8 9.3 %copy-start.19 = (f32[16]{0:T(128)S(1)}, f32[16]{0:T(128)}, u32[]{:S(2)}) copy-start(f32[16]{0:T(128)} %get-tuple-element.1598) | copy-start | bytes 196 | tf_op jit(solution)/shard_map/transpose(jvp())/while
  223.8 9.8 %copy-start.8 = (f32[2,16,128]{2,1,0:T(8,128)S(1)}, f32[2,16,128]{2,1,0:T(8,128)}, u32[]{:S(2)}) copy-start(f32[2,16,128]{2,1,0:T(8,128)} %copy-done.7) | copy-start | bytes 49156 | tf_op jit(solution)/shard_map/transpose(jvp())/while
  233.7 1.2 copy-start.7
  247.9 5.4 %copy-start.2 = (f32[16,128]{1,0:T(8,128)S(1)}, f32[16,128]{1,0:T(8,128)}, u32[]{:S(2)}) copy-start(f32[16,128]{1,0:T(8,128)} %get-tuple-element.1464) | copy-start | bytes 24580 | tf_op jit(solution)/shard_map/transpose(jvp())/while
  247.9 5.4 %copy-start.9 = (f32[16,1]{1,0:T(8,128)S(1)}, f32[16,1]{1,0:T(8,128)}, u32[]{:S(2)}) copy-start(f32[16,1]{1,0:T(8,128)} %get-tuple-element.1466) | copy-start | bytes 196 | tf_op jit(solution)/shard_map/transpose(jvp())/while
  247.9 5.4 %copy-start.10 = (f32[16,1]{1,0:T(8,128)S(1)}, f32[16,1]{1,0:T(8,128)}, u32[]{:S(2)}) copy-start(f32[16,1]{1,0:T(8,128)} %copy.112) | copy-start | bytes 196 | tf_op jit(solution)/shard_map/transpose(jvp())/while
  247.9 5.4 %copy-start.14 = (f32[16]{0:T(128)S(1)}, f32[16]{0:T(128)}, u32[]{:S(2)}) copy-start(f32[16]{0:T(128)} %copy-done.13) | copy-start | bytes 196 | tf_op jit(solution)/shard_map/transpose(jvp())/while
  256.5 11.4 %copy-start.15 = (f32[16]{0:T(128)S(1)}, f32[16]{0:T(128)}, u32[]{:S(2)}) copy-start(f32[16]{0:T(128)} %copy-done.13) | copy-start | bytes 196 | tf_op jit(solution)/shard_map/transpose(jvp())/while
  256.5 11.4 %copy-start.4 = (f32[128,16]{0,1:T(8,128)S(1)}, f32[128,16]{0,1:T(8,128)}, u32[]{:S(2)}) copy-start(f32[128,16]{0,1:T(8,128)} %get-tuple-element.1467) | copy-start | bytes 24580 | tf_op jit(solution)/shard_map/transpose(jvp())/while
  256.5 12.3 %copy-start.5 = (f32[16,128]{1,0:T(8,128)S(1)}, f32[16,128]{1,0:T(8,128)}, u32[]{:S(2)}) copy-start(f32[16,128]{1,0:T(8,128)} %reduce_window_sum.88) | copy-start | bytes 24580 | tf_op jit(solution)/shard_map/transpose(jvp())/while
  259.7 9.2 %copy-start.19 = (f32[16]{0:T(128)S(1)}, f32[16]{0:T(128)}, u32[]{:S(2)}) copy-start(f32[16]{0:T(128)} %get-tuple-element.1598) | copy-start | bytes 196 | tf_op jit(solution)/shard_map/transpose(jvp())/while
  259.7 9.8 %copy-start.8 = (f32[2,16,128]{2,1,0:T(8,128)S(1)}, f32[2,16,128]{2,1,0:T(8,128)}, u32[]{:S(2)}) copy-start(f32[2,16,128]{2,1,0:T(8,128)} %copy-done.7) | copy-start | bytes 49156 | tf_op jit(solution)/shard_map/transpose(jvp())/while
  269.5 31.8 %copy-start.18 = (f32[2,16,128]{2,1,0:T(8,128)S(1)}, f32[2,16,128]{2,1,0:T(8,128)}, u32[]{:S(2)}) copy-start(f32[2,16,128]{2,1,0:T(8,128)} %get-tuple-element.761) | copy-start | bytes 49156
  (8 other events, 5.5 us)
Sparse Core Ops, SparseCore 0:
  13.8 48.7 all-gather.5
  136.9 44.8 all-gather.7
  297.6 15.8 all-reduce.6
where the time goes:
time: 327 us; the launch traced here: 323 us
  local copies, waits for them, and re-layouts  84.5 us (26%)
  waiting for transfers between devices  84.5 us (26%)
  other arithmetic  49.7 us (15%)
  matrix products  46.3 us (14%)
  blocking collectives  40.5 us (12%)
  between operations  16.8 us (5%)
    all_gather x2, waiting for transfers between devices, carried_in(): pieces = jax.tree.map(lambda part: lax.all_gather(part, axis), value)  73 us
    dynamic_update_slice x4, local copies, waits for them, and re-layouts, block_scan(): lax.scan(jax.checkpoint(advance), state_in, (value_blocks, b_blocks, c_bl...  27.8 us
    unnamed x39, local copies, waits for them, and re-layouts  18.7 us
    dot_general x6, matrix products, advance(): inner = jnp.einsum('hij,jhp->ihp', weights, value_blk, precision=HIGHEST)  18.5 us
    unnamed x1, blocking collectives  13.6 us
    psum x1, blocking collectives, local(): lax.psum(jnp.sum(rate_grad * rate_grad) + jnp.sum(gain_grad * gain_grad),...  12.3 us
    psum x1, waiting for transfers between devices, local(): b_grad, c_grad = lax.psum((full_grads[1], full_grads[2]), 'tensor')  11.5 us
    select_n x6, other arithmetic, hop(): jnp.where(position < mine, new, old)  10.3 us
  transfers between devices with their start and end apart: 3, of which 3 were waited for; matrix products, arithmetic and copies ran while one was open for 3% of the time, Pallas kernels for 0%

commit v1 on v0

v1 whole, which is shorter than its diff:
```python
import functools
import jax
import jax.numpy as jnp
from jax import lax
from jax.experimental import pallas as pl
from jax.experimental.pallas import tpu as pltpu
from jax.sharding import PartitionSpec as P

P_SIZE = 64
N = 128
EPSILON = 1e-05
CLIP = 90.0
WIDE = 256
HOP = 128
F32 = jnp.float32
BF16 = jnp.bfloat16
MESH = pl.DeviceIdType.MESH


def nn(a, b):
    return lax.dot_general(a, b, (((1,), (0,)), ((), ())), preferred_element_type=F32)


def nt(a, b):
    return lax.dot_general(a, b, (((1,), (1,)), ((), ())), preferred_element_type=F32)


def split2(x):
    hi = x.astype(BF16)
    return hi, (x - hi.astype(F32)).astype(BF16)


def split3(x):
    hi = x.astype(BF16).astype(F32)
    rest = x - hi
    mid = rest.astype(BF16).astype(F32)
    return hi, mid, rest - mid


def stacked3(x):
    return jnp.concatenate(split3(x), axis=0)


def unstack3(x):
    h = x.shape[0] // 3
    return x[0:h] + x[h : 2 * h] + x[2 * h :]


def kernel(
    sizes,
    v_ref, g_ref, b_ref, c_ref, dt_ref, r_ref, gain_ref, cot_ref,
    res_ref, gv_ref, gg_ref, gb_ref, gc_ref, gs_ref, gr_ref, ggain_ref,
    pex, qex, xhi, xlo, ehi, elo, mix, zd, mte, swi, dsw,
    bx, sin, sout, ce, gin, gout, sq, inn, dm, dca, dba,
    bt, ct, m_hi, m_lo, mt_hi, mt_lo,
    stb, dcb, dbb, gainb, rateb, scb,
    fs, fr, bs, br, st_s, st_r, dc_s, dc_r, db_s, db_r, ga_s, ga_r, ra_s, ra_r, sc_s, sc_r,
):
    n_sec, n_seq, n_ten = sizes
    tokens, channels = v_ref.shape
    heads = dt_ref.shape[0]
    width = WIDE if channels % WIDE == 0 else HOP
    chunks = channels // width
    hops = channels // HOP
    seq = lax.axis_index("seq")
    ten = lax.axis_index("tensor")
    lin = lax.axis_index("section") * n_ten + ten
    n_lin = n_sec * n_ten

    def seq_peer(i):
        return {"seq": i}

    def ten_peer(i):
        return {"tensor": i}

    def lin_peer(i):
        return {"section": i // n_ten, "tensor": i % n_ten}

    barrier = pltpu.get_barrier_semaphore()
    for d in range(1, n_seq):
        pl.semaphore_signal(barrier, inc=1, device_id=seq_peer((seq + d) % n_seq), device_id_type=MESH)
    for d in range(1, n_lin):
        pl.semaphore_signal(barrier, inc=1, device_id=lin_peer((lin + d) % n_lin), device_id_type=MESH)

    def send_all(buf, me, count, peer, ssem, rsem):
        for d in range(1, count):
            pltpu.make_async_remote_copy(
                src_ref=buf.at[me], dst_ref=buf.at[me], send_sem=ssem.at[d - 1], recv_sem=rsem.at[d - 1],
                device_id=peer((me + d) % count), device_id_type=MESH,
            ).start()

    def wait_all(buf, me, count, peer, ssem, rsem):
        for d in range(1, count):
            other = (me + count - d) % count
            desc = pltpu.make_async_remote_copy(
                src_ref=buf.at[me], dst_ref=buf.at[other], send_sem=ssem.at[d - 1], recv_sem=rsem.at[d - 1],
                device_id=peer((me + d) % count), device_id_type=MESH,
            )
            desc.wait_send()
            desc.wait_recv()

    def total_of(buf, count):
        out = buf[0]
        for i in range(1, count):
            out = out + buf[i]
        return out

    def at(c):
        return pl.ds(pl.multiple_of(c * width, width), width)

    def loop(body):
        def step(c, carry):
            body(c, at(c))
            return carry

        lax.fori_loop(0, chunks, step, 0)

    def picks(rows, c):
        row = lax.broadcasted_iota(jnp.int32, (rows, width), 0) & (heads - 1)
        col = lax.broadcasted_iota(jnp.int32, (rows, width), 1) // P_SIZE + c * (width // P_SIZE)
        return jnp.where(row == col, 1.0, 0.0)

    eye = lax.broadcasted_iota(jnp.int32, (heads, heads), 0) == lax.broadcasted_iota(jnp.int32, (heads, heads), 1)
    rate = jnp.sum(jnp.where(eye, r_ref[...], 0.0), axis=1, keepdims=True)
    dt = dt_ref[...]
    row_t = lax.broadcasted_iota(jnp.int32, (tokens, tokens), 0)
    col_t = lax.broadcasted_iota(jnp.int32, (tokens, tokens), 1)
    lower = row_t >= col_t
    upper = row_t <= col_t
    cum = unstack3(nn(stacked3(-dt * rate).astype(BF16), jnp.where(upper, 1.0, 0.0).astype(BF16)))
    p3 = stacked3(jnp.exp(cum)).T.astype(BF16)
    q3 = stacked3(jnp.exp(-cum) * dt).T.astype(BF16)
    bt[...] = b_ref[...].astype(F32).T.astype(BF16)
    ct[...] = c_ref[...].astype(F32).T.astype(BF16)

    def first(c, cols):
        sel = picks(3 * heads, c).astype(BF16)
        pex[:, cols] = nn(p3, sel)
        qx = nn(q3, sel)
        qex[:, cols] = qx
        hi, lo = split2(qx * v_ref[:, cols].astype(F32))
        xhi[:, cols] = hi
        xlo[:, cols] = lo
        bx[:, cols] = nn(bt[...], hi) + nn(bt[...], lo)

    loop(first)

    @pl.when(seq == 0)
    def _():
        sin[...] = jnp.zeros_like(sin)

    @pl.when(seq == n_seq - 1)
    def _():
        gin[...] = jnp.zeros_like(gin)

    pl.semaphore_wait(barrier, n_seq - 1 + n_lin - 1)

    def forward_hop(k):
        cols = pl.ds(k * HOP, HOP)
        return pltpu.make_async_remote_copy(
            src_ref=sout.at[:, cols], dst_ref=sin.at[:, cols], send_sem=fs.at[k], recv_sem=fr.at[k],
            device_id=seq_peer((seq + 1) % n_seq), device_id_type=MESH,
        )

    def backward_hop(k):
        cols = pl.ds(k * HOP, HOP)
        return pltpu.make_async_remote_copy(
            src_ref=gout.at[:, cols], dst_ref=gin.at[:, cols], send_sem=bs.at[k], recv_sem=br.at[k],
            device_id=seq_peer((seq + n_seq - 1) % n_seq), device_id_type=MESH,
        )

    def total_decay(cols):
        return pex[tokens - 1 : tokens, cols]

    @pl.when(seq == 0)
    def _():
        for k in range(hops):
            cols = pl.ds(k * HOP, HOP)
            sout[:, cols] = total_decay(cols) * bx[:, cols]
            forward_hop(k).start()

    cb = nt(c_ref[...], b_ref[...])
    hi, lo = split2(jnp.where(lower, cb, 0.0))
    m_hi[...] = hi
    m_lo[...] = lo
    bc = nt(b_ref[...], c_ref[...])
    hi, lo = split2(jnp.where(upper, bc, 0.0))
    mt_hi[...] = hi
    mt_lo[...] = lo

    def second(c, cols):
        gate = g_ref[:, cols].astype(F32)
        sigm = 1.0 / (1.0 + jnp.exp(-gate))
        swi[:, cols] = gate * sigm
        dsw[:, cols] = sigm * (1.0 + gate * (1.0 - sigm))
        x_hi = xhi[:, cols]
        mix[:, cols] = nn(m_hi[...], x_hi) + (nn(m_hi[...], xlo[:, cols]) + nn(m_lo[...], x_hi))

    loop(second)

    @pl.when(seq > 0)
    def _():
        for k in range(hops):
            cols = pl.ds(k * HOP, HOP)
            forward_hop(k).wait_recv()

            @pl.when(seq < n_seq - 1)
            def _():
                sout[:, cols] = total_decay(cols) * (sin[:, cols] + bx[:, cols])
                forward_hop(k).start()

    sq[...] = jnp.zeros_like(sq)
    inn[...] = jnp.zeros_like(inn)

    def third(c, cols):
        hi, lo = split2(sin[:, cols])
        mixed = pex[:, cols] * (mix[:, cols] + (nn(c_ref[...], hi) + nn(c_ref[...], lo)))
        mix[:, cols] = mixed
        gated = mixed * swi[:, cols]
        squares = gated * gated
        products = cot_ref[:, cols].astype(F32) * gain_ref[:, cols] * gated
        for part in range(width // HOP):
            piece = slice(part * HOP, (part + 1) * HOP)
            sq[...] += squares[:, piece]
            inn[...] += products[:, piece]

    loop(third)

    lane = lax.broadcasted_iota(jnp.int32, (tokens, 128), 1)
    stb[ten] = jnp.where(
        lane < 64, jnp.sum(sq[...], axis=1, keepdims=True), jnp.sum(inn[...], axis=1, keepdims=True)
    )
    send_all(stb, ten, n_ten, ten_peer, st_s, st_r)
    wait_all(stb, ten, n_ten, ten_peer, st_s, st_r)
    sums = total_of(stb, n_ten)
    group_width = channels * n_ten
    scale = lax.rsqrt(sums[:, 0:1] / group_width + EPSILON)
    pull = scale * scale * scale * sums[:, 64:65] / group_width

    def fourth(c, cols):
        mixed = mix[:, cols]
        swish = swi[:, cols]
        gated = mixed * swish
        d_gated = scale * (cot_ref[:, cols].astype(F32) * gain_ref[:, cols]) - gated * pull
        gg_ref[:, cols] = (d_gated * mixed * dsw[:, cols]).astype(BF16)
        d_mixed = d_gated * swish
        zd[:, cols] = d_mixed * mixed
        hi, lo = split2(pex[:, cols] * d_mixed)
        ehi[:, cols] = hi
        elo[:, cols] = lo
        ce[:, cols] = nn(ct[...], hi) + nn(ct[...], lo)

    loop(fourth)

    @pl.when(seq == n_seq - 1)
    def _():
        for k in range(hops):
            cols = pl.ds(k * HOP, HOP)
            gout[:, cols] = ce[:, cols]
            backward_hop(k).start()

    dm[...] = jnp.zeros_like(dm)
    dca[...] = jnp.zeros_like(dca)

    def fifth(c, cols):
        e_hi = ehi[:, cols]
        e_lo = elo[:, cols]
        x_hi = xhi[:, cols]
        mte[:, cols] = nn(mt_hi[...], e_hi) + (nn(mt_hi[...], e_lo) + nn(mt_lo[...], e_hi))
        dm[...] += nt(e_hi, x_hi) + (nt(e_hi, xlo[:, cols]) + nt(e_lo, x_hi))
        s_hi, s_lo = split2(sin[:, cols])
        dca[...] += nt(e_hi, s_hi) + (nt(e_hi, s_lo) + nt(e_lo, s_hi))
        normed = mix[:, cols] * swi[:, cols] * scale
        res_ref[:, cols] = (normed * gain_ref[:, cols]).astype(BF16)
        gain_sum = jnp.sum(cot_ref[:, cols].astype(F32) * normed, axis=0, keepdims=True)
        gainb[seq, :, cols] = jnp.broadcast_to(gain_sum, (8, width))

    loop(fifth)
    send_all(gainb, seq, n_seq, seq_peer, ga_s, ga_r)
    d_m = jnp.where(lower, dm[...], 0.0)
    hi, lo = split2(d_m)
    dcb[ten] = dca[...] + (nn(hi, b_ref[...]) + nn(lo, b_ref[...]))
    send_all(dcb, ten, n_ten, ten_peer, dc_s, dc_r)
    hi, lo = split2(d_m.T)
    dba[...] = nn(hi, c_ref[...]) + nn(lo, c_ref[...])

    @pl.when(seq < n_seq - 1)
    def _():
        for k in range(hops):
            cols = pl.ds(k * HOP, HOP)
            backward_hop(k).wait_recv()

            @pl.when(seq > 0)
            def _():
                gout[:, cols] = ce[:, cols] + total_decay(cols) * gin[:, cols]
                backward_hop(k).start()

    def sixth(c, carry):
        cols = at(c)
        row_sum, direct, end = carry
        e_grad = total_decay(cols) * gin[:, cols]
        hi, lo = split2(e_grad)
        d_v = qex[:, cols] * (mte[:, cols] + (nn(b_ref[...], hi) + nn(b_ref[...], lo)))
        gv_ref[:, cols] = d_v.astype(BF16)
        x_hi = xhi[:, cols]
        dba[...] += nt(x_hi, hi) + (nt(x_hi, lo) + nt(xlo[:, cols], hi))
        own = d_v * v_ref[:, cols].astype(F32)
        sel = picks(heads, c)
        pick = sel.astype(BF16)
        a, b, d = split3(zd[:, cols] - own)
        row_sum = row_sum + (nt(pick, a.astype(BF16)) + nt(pick, b.astype(BF16)) + nt(pick, d.astype(BF16)))
        hi, lo = split2(own)
        direct = direct + (nt(pick, hi) + nt(pick, lo))
        column = jnp.sum(e_grad * (sin[:, cols] + bx[:, cols]), axis=0, keepdims=True)
        end = end + jnp.sum(sel * column, axis=1, keepdims=True)
        return row_sum, direct, end

    zero = jnp.zeros((heads, tokens), F32)
    row_sum, direct, end = lax.fori_loop(0, chunks, sixth, (zero, zero, jnp.zeros((heads, 1), F32)))
    dbb[ten] = dba[...]
    send_all(dbb, ten, n_ten, ten_peer, db_s, db_r)
    tail = unstack3(nn(stacked3(row_sum).astype(BF16), jnp.where(lower, 1.0, 0.0).astype(BF16))) + end
    rateb[seq] = jnp.broadcast_to(-jnp.sum(dt * tail, axis=1, keepdims=True), (heads, 128))
    send_all(rateb, seq, n_seq, seq_peer, ra_s, ra_r)
    gs_ref[...] = direct / dt - rate * tail
    wait_all(gainb, seq, n_seq, seq_peer, ga_s, ga_r)
    gain_total = total_of(gainb, n_seq)[0:1]
    gain_square = jnp.sum(gain_total * gain_total, axis=1, keepdims=True)
    wait_all(rateb, seq, n_seq, seq_peer, ra_s, ra_r)
    rate_total = total_of(rateb, n_seq)
    scb[lin] = jnp.broadcast_to(jnp.sum(rate_total * rate_total, axis=0, keepdims=True) + gain_square, (8, 128))
    send_all(scb, lin, n_lin, lin_peer, sc_s, sc_r)
    wait_all(dcb, ten, n_ten, ten_peer, dc_s, dc_r)
    gc_ref[...] = total_of(dcb, n_ten)
    wait_all(dbb, ten, n_ten, ten_peer, db_s, db_r)
    gb_ref[...] = total_of(dbb, n_ten)

    @pl.when(seq < n_seq - 1)
    def _():
        for k in range(hops):
            forward_hop(k).wait_send()

    @pl.when(seq > 0)
    def _():
        for k in range(hops):
            backward_hop(k).wait_send()

    wait_all(scb, lin, n_lin, lin_peer, sc_s, sc_r)
    total = total_of(scb, n_lin)
    factor = CLIP / jnp.maximum(jnp.sqrt(total), CLIP)
    ggain_ref[...] = gain_total * factor[0:1, 0:1]
    line = lax.broadcasted_iota(jnp.int32, (heads, 128), 0) == lax.broadcasted_iota(jnp.int32, (heads, 128), 1)
    gr_ref[...] = jnp.sum(jnp.where(line, rate_total * factor[0:1], 0.0), axis=0, keepdims=True)


def local(values, gate_in, b_proj, c_proj, step_size, decay_rate, norm_gain, cotangent):
    n_sec, n_seq, n_ten = lax.axis_size("section"), lax.axis_size("seq"), lax.axis_size("tensor")
    n_lin = n_sec * n_ten
    tokens, channels = values.shape
    heads = decay_rate.shape[0]
    hops = channels // HOP
    shape = jax.ShapeDtypeStruct
    vm = pltpu.VMEM
    wide32 = vm((tokens, channels), F32)
    wide16 = vm((tokens, channels), BF16)
    state = vm((N, channels), F32)
    square16 = vm((tokens, tokens), BF16)
    slim = vm((tokens, 128), F32)
    sems = pltpu.SemaphoreType.DMA
    outs = pl.pallas_call(
        functools.partial(kernel, (n_sec, n_seq, n_ten)),
        out_shape=(
            shape((tokens, channels), BF16),
            shape((tokens, channels), BF16),
            shape((tokens, channels), BF16),
            shape((tokens, N), F32),
            shape((tokens, N), F32),
            shape((heads, tokens), F32),
            shape((1, 128), F32),
            shape((1, channels), F32),
        ),
        in_specs=[pl.BlockSpec(memory_space=vm)] * 8,
        out_specs=[pl.BlockSpec(memory_space=vm)] * 8,
        scratch_shapes=[
            wide32, wide32, wide16, wide16, wide16, wide16, wide32, wide32, wide32, wide32, wide32,
            state, state, state, state, state, state, slim, slim, vm((tokens, tokens), F32), slim, slim,
            vm((N, tokens), BF16), vm((N, tokens), BF16), square16, square16, square16, square16,
            vm((n_ten, tokens, 128), F32), vm((n_ten, tokens, 128), F32), vm((n_ten, tokens, 128), F32),
            vm((n_seq, 8, channels), F32), vm((n_seq, heads, 128), F32), vm((n_lin, 8, 128), F32),
            sems((hops,)), sems((hops,)), sems((hops,)), sems((hops,)),
            sems((n_ten,)), sems((n_ten,)), sems((n_ten,)), sems((n_ten,)), sems((n_ten,)), sems((n_ten,)),
            sems((n_seq,)), sems((n_seq,)), sems((n_seq,)), sems((n_seq,)), sems((n_lin,)), sems((n_lin,)),
        ],
        compiler_params=pltpu.CompilerParams(
            collective_id=0, has_side_effects=True, vmem_limit_bytes=48 * 1024 * 1024
        ),
    )(
        values, gate_in, b_proj[:, 0, :], c_proj[:, 0, :], step_size,
        decay_rate[None, :], norm_gain[None, :], cotangent,
    )
    result, grad_values, grad_gate, grad_b, grad_c, grad_step, grad_rate, grad_gain = outs
    return (
        result, grad_values, grad_gate, grad_b[:, None, :], grad_c[:, None, :], grad_step,
        grad_rate[0, :heads], grad_gain[0],
    )


def solution(mesh):
    return jax.shard_map(
        local,
        mesh=mesh,
        in_specs=(
            P("seq", ("section", "tensor")),
            P("seq", ("section", "tensor")),
            P("seq", "section", None),
            P("seq", "section", None),
            P(("section", "tensor"), "seq"),
            P(("section", "tensor")),
            P(("section", "tensor")),
            P("seq", ("section", "tensor")),
        ),
        out_specs=(
            P("seq", ("section", "tensor")),
            P("seq", ("section", "tensor")),
            P("seq", ("section", "tensor")),
            P("seq", "section", None),
            P("seq", "section", None),
            P(("section", "tensor"), "seq"),
            P(("section", "tensor")),
            P(("section", "tensor")),
        ),
        check_vma=False,
    )
```

time: 327 us -> 73.9 us (0.23); the launches traced: 323 us -> 73.4 us
  waiting for transfers between devices: 84.5 us -> 0 us
  local copies, waits for them, and re-layouts: 84.5 us -> 11.6 us
  Pallas kernels: 0 us -> 61.2 us
  other arithmetic: 49.7 us -> 0 us
  matrix products: 46.3 us -> 0 us
  blocking collectives: 40.5 us -> 0 us
  between operations: 16.8 us -> 0.67 us
    all_gather x2 -> x0, waiting for transfers between devices: 73 us -> none  [carried_in(): pieces = jax.tree.map(lambda part: lax.all_gather(part, axis), value)]
    pallas_call x0 -> x1, Pallas kernels: none -> 61.2 us  [local(): pl.pallas_call(functools.partial(kernel, (n_sec, n_seq, n_ten)), out_shap...]
    dot_general x27 -> x0, matrix products: 44 us -> none  [the longest x6 18.5 us: advance(): inner = jnp.einsum('hij,jhp->ihp', weights, value_blk, precision=HIGHEST)]
    dynamic_update_slice x4 -> x0, local copies, waits for them, and re-layouts: 27.8 us -> none  [block_scan(): lax.scan(jax.checkpoint(advance), state_in, (value_blocks, b_blocks, c_bl...]
    psum x4 -> x0, blocking collectives: 27 us -> none  [the longest x1 12.3 us: local(): lax.psum(jnp.sum(rate_grad * rate_grad) + jnp.sum(gain_grad * gain_grad),...]
    mul x13 -> x0, other arithmetic: 14.6 us -> none  [the longest x6 5.58 us: advance(): cumulative = jnp.cumsum(-dt_blk * rates[:, None], axis=1)]
    unnamed x1 -> x0, blocking collectives: 13.6 us -> none
    psum x1 -> x0, waiting for transfers between devices: 11.5 us -> none  [local(): b_grad, c_grad = lax.psum((full_grads[1], full_grads[2]), 'tensor')]
  transfers between devices with their start and end apart: 3 -> 0, of which waited for: 3 -> 0; matrix products, arithmetic and copies ran while one was open for 3% -> 0% of each run, Pallas kernels for 0% -> 0%
where the time goes in v1:
time: 73.9 us; the launch traced here: 73.4 us
  Pallas kernels  61.2 us (83%)
  local copies, waits for them, and re-layouts  11.6 us (16%)
    pallas_call x1, Pallas kernels, local(): pl.pallas_call(functools.partial(kernel, (n_sec, n_seq, n_ten)), out_shap...  61.2 us
    unnamed x23, local copies, waits for them, and re-layouts  11.1 us

profile of v1, /device:TPU:0, one launch (start us, length us, event | category | flops | bytes accessed | tf_op | source)
XLA Modules:
  0.0 73.4 jit_solution(9504350537399849990)
XLA Ops:
  0.6 0.0 copy-start.6
  0.6 0.0 copy-start.7
  0.7 0.7 copy-done.6
  1.3 0.0 copy-done.7
  1.3 0.0 copy-start
  1.3 1.0 %copy-done = bf16[256,1024]{1,0:T(8,128)(2,1)S(1)} copy-done((bf16[256,1024]{1,0:T(8,128)(2,1)S(1)}, bf16[256,1024]{1,0:T(8,128)(2,1)}, u32[]{:S(2)}) %copy-start) | copy-done | bytes 524312
  2.4 0.0 copy-start.1
  2.4 1.0 %copy-done.1 = bf16[256,1024]{1,0:T(8,128)(2,1)S(1)} copy-done((bf16[256,1024]{1,0:T(8,128)(2,1)S(1)}, bf16[256,1024]{1,0:T(8,128)(2,1)}, u32[]{:S(2)}) %copy-start.1) | copy-done | bytes 524312
  3.4 0.0 copy-start.2
  3.4 1.0 %copy-done.2 = bf16[256,1024]{1,0:T(8,128)(2,1)S(1)} copy-done((bf16[256,1024]{1,0:T(8,128)(2,1)S(1)}, bf16[256,1024]{1,0:T(8,128)(2,1)}, u32[]{:S(2)}) %copy-start.2) | copy-done | bytes 524312
  4.5 0.0 copy-start.3
  4.5 0.8 %copy-done.3 = bf16[256,1,128]{2,0,1:T(8,128)(2,1)S(1)} copy-done((bf16[256,1,128]{2,0,1:T(8,128)(2,1)S(1)}, bf16[256,1,128]{2,0,1:T(8,128)(2,1)}, u32[]{:S(2)}) %copy-start.3) | copy-done | bytes 65560
  5.3 0.0 copy-start.4
  5.3 0.8 %copy-done.4 = bf16[256,1,128]{2,0,1:T(8,128)(2,1)S(1)} copy-done((bf16[256,1,128]{2,0,1:T(8,128)(2,1)S(1)}, bf16[256,1,128]{2,0,1:T(8,128)(2,1)}, u32[]{:S(2)}) %copy-start.4) | copy-done | bytes 65560
  6.1 0.0 copy-start.5
  6.1 0.7 copy-done.5
  6.9 61.2 %shard_map.143 = (bf16[256,1024]{1,0:T(8,128)(2,1)S(1)}, bf16[256,1024]{1,0:T(8,128)(2,1)S(1)}, bf16[256,1024]{1,0:T(8,128)(2,1)S(1)}, f32[256,128]{1,0:T(8,128)...) custom-call(bf16[256,1024]{1,0:T(8,128)(2,1)S(1)} %copy-done, ...), custom_call_target="tpu_custom_call" | custom-call | tf_op jit(solution)/shard_map/pallas_call | solution.py:370
  68.0 0.5 slice_bitcast_fusion
  68.6 0.8 %copy.25 = bf16[256,1024]{1,0:T(8,128)(2,1)} copy(bf16[256,1024]{1,0:T(8,128)(2,1)S(1)} %get-tuple-element.40) | data formatting | bytes 1048576
  69.3 0.8 %copy.26 = bf16[256,1024]{1,0:T(8,128)(2,1)} copy(bf16[256,1024]{1,0:T(8,128)(2,1)S(1)} %get-tuple-element.41) | data formatting | bytes 1048576
  70.1 0.8 %copy.27 = bf16[256,1024]{1,0:T(8,128)(2,1)} copy(bf16[256,1024]{1,0:T(8,128)(2,1)S(1)} %get-tuple-element.42) | data formatting | bytes 1048576
  70.9 0.7 copy.28
  71.6 0.7 copy.29
  72.2 0.6 copy.30
  72.9 0.6 copy.31
Async XLA Ops:
  0.6 0.7 copy-start.6
  0.6 0.7 copy-start.7
  1.3 1.0 %copy-start = (bf16[256,1024]{1,0:T(8,128)(2,1)S(1)}, bf16[256,1024]{1,0:T(8,128)(2,1)}, u32[]{:S(2)}) copy-start(bf16[256,1024]{1,0:T(8,128)(2,1)} %v_ref.1) | copy-start | bytes 1572868
  2.4 1.0 %copy-start.1 = (bf16[256,1024]{1,0:T(8,128)(2,1)S(1)}, bf16[256,1024]{1,0:T(8,128)(2,1)}, u32[]{:S(2)}) copy-start(bf16[256,1024]{1,0:T(8,128)(2,1)} %g_ref.1) | copy-start | bytes 1572868
  3.4 1.0 %copy-start.2 = (bf16[256,1024]{1,0:T(8,128)(2,1)S(1)}, bf16[256,1024]{1,0:T(8,128)(2,1)}, u32[]{:S(2)}) copy-start(bf16[256,1024]{1,0:T(8,128)(2,1)} %cot_ref.1) | copy-start | bytes 1572868
  4.5 0.8 %copy-start.3 = (bf16[256,1,128]{2,0,1:T(8,128)(2,1)S(1)}, bf16[256,1,128]{2,0,1:T(8,128)(2,1)}, u32[]{:S(2)}) copy-start(bf16[256,1,128]{2,0,1:T(8,128)(2,1)} %param.10) | copy-start | bytes 196612
  5.3 0.8 %copy-start.4 = (bf16[256,1,128]{2,0,1:T(8,128)(2,1)S(1)}, bf16[256,1,128]{2,0,1:T(8,128)(2,1)}, u32[]{:S(2)}) copy-start(bf16[256,1,128]{2,0,1:T(8,128)(2,1)} %param.11) | copy-start | bytes 196612
  6.1 0.7 copy-start.5

commit v2 on v1

--- a/solution.py
+++ b/solution.py
@@ -48,12 +48,13 @@
 
 def kernel(
     sizes,
-    v_ref, g_ref, b_ref, c_ref, dt_ref, r_ref, gain_ref, cot_ref,
+    v_in, g_in, b_in, c_in, dt_in, r_in, gain_in, cot_in,
     res_ref, gv_ref, gg_ref, gb_ref, gc_ref, gs_ref, gr_ref, ggain_ref,
     pex, qex, xhi, xlo, ehi, elo, mix, zd, mte, swi, dsw,
     bx, sin, sout, ce, gin, gout, sq, inn, dm, dca, dba,
     bt, ct, m_hi, m_lo, mt_hi, mt_lo,
     stb, dcb, dbb, gainb, rateb, scb,
+    v_ref, g_ref, b_ref, c_ref, dt_ref, r_ref, gain_ref, cot_ref, loads,
     fs, fr, bs, br, st_s, st_r, dc_s, dc_r, db_s, db_r, ga_s, ga_r, ra_s, ra_r, sc_s, sc_r,
 ):
     n_sec, n_seq, n_ten = sizes
@@ -76,6 +77,16 @@
     def lin_peer(i):
         return {"section": i // n_ten, "tensor": i % n_ten}
 
+    def load(i, src, dst):
+        return pltpu.make_async_copy(src, dst, loads.at[i])
+
+    load_small = [
+        load(0, dt_in, dt_ref), load(1, r_in, r_ref), load(2, b_in, b_ref), load(3, c_in, c_ref),
+    ]
+    load_values = load(4, v_in, v_ref)
+    load_late = [load(5, g_in, g_ref), load(6, cot_in, cot_ref), load(7, gain_in, gain_ref)]
+    for copy in load_small + [load_values] + load_late:
+        copy.start()
     barrier = pltpu.get_barrier_semaphore()
     for d in range(1, n_seq):
         pl.semaphore_signal(barrier, inc=1, device_id=seq_peer((seq + d) % n_seq), device_id_type=MESH)
@@ -120,6 +131,8 @@
         col = lax.broadcasted_iota(jnp.int32, (rows, width), 1) // P_SIZE + c * (width // P_SIZE)
         return jnp.where(row == col, 1.0, 0.0)
 
+    for copy in load_small:
+        copy.wait()
     eye = lax.broadcasted_iota(jnp.int32, (heads, heads), 0) == lax.broadcasted_iota(jnp.int32, (heads, heads), 1)
     rate = jnp.sum(jnp.where(eye, r_ref[...], 0.0), axis=1, keepdims=True)
     dt = dt_ref[...]
@@ -133,6 +146,27 @@
     bt[...] = b_ref[...].astype(F32).T.astype(BF16)
     ct[...] = c_ref[...].astype(F32).T.astype(BF16)
 
+    def forward_hop(k):
+        cols = pl.ds(pl.multiple_of(k * HOP, HOP), HOP)
+        return pltpu.make_async_remote_copy(
+            src_ref=sout.at[:, cols], dst_ref=sin.at[:, cols], send_sem=fs.at[k], recv_sem=fr.at[k],
+            device_id=seq_peer((seq + 1) % n_seq), device_id_type=MESH,
+        )
+
+    def backward_hop(k):
+        cols = pl.ds(pl.multiple_of(k * HOP, HOP), HOP)
+        return pltpu.make_async_remote_copy(
+            src_ref=gout.at[:, cols], dst_ref=gin.at[:, cols], send_sem=bs.at[k], recv_sem=br.at[k],
+            device_id=seq_peer((seq + n_seq - 1) % n_seq), device_id_type=MESH,
+        )
+
+    def total_decay(cols):
+        return pex[tokens - 1 : tokens, cols]
+
+    def hops_of(c):
+        per = width // HOP
+        return [(c * per + i, pl.ds(pl.multiple_of((c * per + i) * HOP, HOP), HOP)) for i in range(per)]
+
     def first(c, cols):
         sel = picks(3 * heads, c).astype(BF16)
         pex[:, cols] = nn(p3, sel)
@@ -143,6 +177,14 @@
         xlo[:, cols] = lo
         bx[:, cols] = nn(bt[...], hi) + nn(bt[...], lo)
 
+        @pl.when(seq == 0)
+        def _():
+            for k, part in hops_of(c):
+                sout[:, part] = total_decay(part) * bx[:, part]
+                forward_hop(k).start()
+
+    load_values.wait()
+    pl.semaphore_wait(barrier, n_seq - 1 + n_lin - 1)
     loop(first)
 
     @pl.when(seq == 0)
@@ -152,32 +194,6 @@
     @pl.when(seq == n_seq - 1)
     def _():
         gin[...] = jnp.zeros_like(gin)
-
-    pl.semaphore_wait(barrier, n_seq - 1 + n_lin - 1)
-
-    def forward_hop(k):
-        cols = pl.ds(k * HOP, HOP)
-        return pltpu.make_async_remote_copy(
-            src_ref=sout.at[:, cols], dst_ref=sin.at[:, cols], send_sem=fs.at[k], recv_sem=fr.at[k],
-            device_id=seq_peer((seq + 1) % n_seq), device_id_type=MESH,
-        )
-
-    def backward_hop(k):
-        cols = pl.ds(k * HOP, HOP)
-        return pltpu.make_async_remote_copy(
-            src_ref=gout.at[:, cols], dst_ref=gin.at[:, cols], send_sem=bs.at[k], recv_sem=br.at[k],
-            device_id=seq_peer((seq + n_seq - 1) % n_seq), device_id_type=MESH,
-        )
-
-    def total_decay(cols):
-        return pex[tokens - 1 : tokens, cols]
-
-    @pl.when(seq == 0)
-    def _():
-        for k in range(hops):
-            cols = pl.ds(k * HOP, HOP)
-            sout[:, cols] = total_decay(cols) * bx[:, cols]
-            forward_hop(k).start()
 
     cb = nt(c_ref[...], b_ref[...])
     hi, lo = split2(jnp.where(lower, cb, 0.0))
@@ -196,23 +212,24 @@
         x_hi = xhi[:, cols]
         mix[:, cols] = nn(m_hi[...], x_hi) + (nn(m_hi[...], xlo[:, cols]) + nn(m_lo[...], x_hi))
 
+    for copy in load_late:
+        copy.wait()
     loop(second)
-
-    @pl.when(seq > 0)
-    def _():
-        for k in range(hops):
-            cols = pl.ds(k * HOP, HOP)
-            forward_hop(k).wait_recv()
-
-            @pl.when(seq < n_seq - 1)
-            def _():
-                sout[:, cols] = total_decay(cols) * (sin[:, cols] + bx[:, cols])
-                forward_hop(k).start()
 
     sq[...] = jnp.zeros_like(sq)
     inn[...] = jnp.zeros_like(inn)
 
     def third(c, cols):
+        @pl.when(seq > 0)
+        def _():
+            for k, part in hops_of(c):
+                forward_hop(k).wait_recv()
+
+                @pl.when(seq < n_seq - 1)
+                def _():
+                    sout[:, part] = total_decay(part) * (sin[:, part] + bx[:, part])
+                    forward_hop(k).start()
+
         hi, lo = split2(sin[:, cols])
         mixed = pex[:, cols] * (mix[:, cols] + (nn(c_ref[...], hi) + nn(c_ref[...], lo)))
         mix[:, cols] = mixed
@@ -250,14 +267,13 @@
         elo[:, cols] = lo
         ce[:, cols] = nn(ct[...], hi) + nn(ct[...], lo)
 
+        @pl.when(seq == n_seq - 1)
+        def _():
+            for k, part in hops_of(c):
+                gout[:, part] = ce[:, part]
+                backward_hop(k).start()
+
     loop(fourth)
-
-    @pl.when(seq == n_seq - 1)
-    def _():
-        for k in range(hops):
-            cols = pl.ds(k * HOP, HOP)
-            gout[:, cols] = ce[:, cols]
-            backward_hop(k).start()
 
     dm[...] = jnp.zeros_like(dm)
     dca[...] = jnp.zeros_like(dca)
@@ -284,20 +300,20 @@
     hi, lo = split2(d_m.T)
     dba[...] = nn(hi, c_ref[...]) + nn(lo, c_ref[...])
 
-    @pl.when(seq < n_seq - 1)
-    def _():
-        for k in range(hops):
-            cols = pl.ds(k * HOP, HOP)
-            backward_hop(k).wait_recv()
-
-            @pl.when(seq > 0)
-            def _():
-                gout[:, cols] = ce[:, cols] + total_decay(cols) * gin[:, cols]
-                backward_hop(k).start()
-
     def sixth(c, carry):
         cols = at(c)
         row_sum, direct, end = carry
+
+        @pl.when(seq < n_seq - 1)
+        def _():
+            for k, part in hops_of(c):
+                backward_hop(k).wait_recv()
+
+                @pl.when(seq > 0)
+                def _():
+                    gout[:, part] = ce[:, part] + total_decay(part) * gin[:, part]
+                    backward_hop(k).start()
+
         e_grad = total_decay(cols) * gin[:, cols]
         hi, lo = split2(e_grad)
         d_v = qex[:, cols] * (mte[:, cols] + (nn(b_ref[...], hi) + nn(b_ref[...], lo)))
@@ -349,8 +365,20 @@
     total = total_of(scb, n_lin)
     factor = CLIP / jnp.maximum(jnp.sqrt(total), CLIP)
     ggain_ref[...] = gain_total * factor[0:1, 0:1]
-    line = lax.broadcasted_iota(jnp.int32, (heads, 128), 0) == lax.broadcasted_iota(jnp.int32, (heads, 128), 1)
-    gr_ref[...] = jnp.sum(jnp.where(line, rate_total * factor[0:1], 0.0), axis=0, keepdims=True)
+    gr_ref[...] = jnp.sum(jnp.where(eye, (rate_total * factor[0:1])[:, 0:heads], 0.0), axis=0, keepdims=True)
+
+
+def write_out(*refs):
+    here, arrived, done = refs[16:24], refs[24], refs[25]
+    loads = [pltpu.make_async_copy(refs[i], here[i], arrived.at[i]) for i in range(8)]
+    stores = [pltpu.make_async_copy(here[i], refs[8 + i], done.at[i]) for i in range(8)]
+    for load in loads:
+        load.start()
+    for load, store in zip(loads, stores):
+        load.wait()
+        store.start()
+    for store in stores:
+        store.wait()
 
 
 def local(values, gate_in, b_proj, c_proj, step_size, decay_rate, norm_gain, cotangent):
@@ -376,10 +404,10 @@
             shape((tokens, N), F32),
             shape((tokens, N), F32),
             shape((heads, tokens), F32),
-            shape((1, 128), F32),
+            shape((1, heads), F32),
             shape((1, channels), F32),
         ),
-        in_specs=[pl.BlockSpec(memory_space=vm)] * 8,
+        in_specs=[pl.BlockSpec(memory_space=pltpu.HBM)] * 8,
         out_specs=[pl.BlockSpec(memory_space=vm)] * 8,
         scratch_shapes=[
             wide32, wide32, wide16, wide16, wide16, wide16, wide32, wide32, wide32, wide32, wide32,
@@ -387,21 +415,31 @@
             vm((N, tokens), BF16), vm((N, tokens), BF16), square16, square16, square16, square16,
             vm((n_ten, tokens, 128), F32), vm((n_ten, tokens, 128), F32), vm((n_ten, tokens, 128), F32),
             vm((n_seq, 8, channels), F32), vm((n_seq, heads, 128), F32), vm((n_lin, 8, 128), F32),
+            vm((tokens, channels), BF16), vm((tokens, channels), BF16), vm((tokens, N), BF16), vm((tokens, N), BF16),
+            vm((heads, tokens), F32), vm((1, heads), F32), vm((1, channels), F32), vm((tokens, channels), BF16),
+            sems((8,)),
             sems((hops,)), sems((hops,)), sems((hops,)), sems((hops,)),
             sems((n_ten,)), sems((n_ten,)), sems((n_ten,)), sems((n_ten,)), sems((n_ten,)), sems((n_ten,)),
             sems((n_seq,)), sems((n_seq,)), sems((n_seq,)), sems((n_seq,)), sems((n_lin,)), sems((n_lin,)),
         ],
         compiler_params=pltpu.CompilerParams(
-            collective_id=0, has_side_effects=True, vmem_limit_bytes=48 * 1024 * 1024
+            collective_id=0, has_side_effects=True, vmem_limit_bytes=56 * 1024 * 1024
         ),
     )(
         values, gate_in, b_proj[:, 0, :], c_proj[:, 0, :], step_size,
         decay_rate[None, :], norm_gain[None, :], cotangent,
     )
-    result, grad_values, grad_gate, grad_b, grad_c, grad_step, grad_rate, grad_gain = outs
+    result, grad_values, grad_gate, grad_b, grad_c, grad_step, grad_rate, grad_gain = pl.pallas_call(
+        write_out,
+        out_shape=tuple(shape(x.shape, x.dtype) for x in outs),
+        in_specs=[pl.BlockSpec(memory_space=pl.ANY)] * 8,
+        out_specs=[pl.BlockSpec(memory_space=pl.ANY)] * 8,
+        scratch_shapes=[vm(x.shape, x.dtype) for x in outs] + [sems((8,)), sems((8,))],
+        compiler_params=pltpu.CompilerParams(vmem_limit_bytes=56 * 1024 * 1024),
+    )(*outs)
     return (
         result, grad_values, grad_gate, grad_b[:, None, :], grad_c[:, None, :], grad_step,
-        grad_rate[0, :heads], grad_gain[0],
+        grad_rate[0], grad_gain[0],
     )
 
 

time: 73.9 us -> 62.6 us (0.85)
  local copies, waits for them, and re-layouts: 11.6 us -> 0 us
    unnamed x23 -> x0, local copies, waits for them, and re-layouts: 11.1 us -> none
    pallas_call x0 -> x1, Pallas kernels: none -> 2.41 us  [local(): pl.pallas_call(write_out, out_shape=tuple((shape(x.shape, x.dtype) for x...]
    pallas_call x1, Pallas kernels: 61.2 us -> 59.4 us  [local(): pl.pallas_call(functools.partial(kernel, (n_sec, n_seq, n_ten)), out_shap...]
where the time goes in v2:
time: 62.6 us; the launch traced here: 62.4 us
  Pallas kernels  61.8 us (99%)
  between operations  0.64 us (1%)
    pallas_call x1, Pallas kernels, local(): pl.pallas_call(functools.partial(kernel, (n_sec, n_seq, n_ten)), out_shap...  59.4 us
    pallas_call x1, Pallas kernels, local(): pl.pallas_call(write_out, out_shape=tuple((shape(x.shape, x.dtype) for x...  2.41 us

profile of v2, /device:TPU:0, one launch (start us, length us, event | category | flops | bytes accessed | tf_op | source)
XLA Modules:
  0.0 62.4 jit_solution(14154408936077206090)
XLA Ops:
  0.6 59.4 %shard_map.143 = (bf16[256,1024]{1,0:T(8,128)(2,1)}, bf16[256,1024]{1,0:T(8,128)(2,1)}, bf16[256,1024]{1,0:T(8,128)(2,1)}, f32[256,128]{1,0:T(8,128)}, f32[256,1...) custom-call(bf16[256,1024]{1,0:T(8,128)(2,1)} %v_in.1, bf16[256,1024]{1,0:T(8,128)(2,1)} %g_in.1, ...), custom_call_target="tpu_custom_call" | custom-call | tf_op jit(solution)/shard_map/pallas_call | solution.py:398
  60.0 2.4 %shard_map.144 = (bf16[256,1024]{1,0:T(8,128)(2,1)}, bf16[256,1024]{1,0:T(8,128)(2,1)}, bf16[256,1024]{1,0:T(8,128)(2,1)}, f32[256,128]{1,0:T(8,128)}, f32[256,1...) custom-call(bf16[256,1024]{1,0:T(8,128)(2,1)} %get-tuple-element.24.refs_0_, ...), custom_call_target="tpu_custom_call" | custom-call | tf_op jit(solution)/shard_map/pallas_call | solution.py:432

commit v3 on v2

--- a/solution.py
+++ b/solution.py
@@ -12,6 +12,7 @@
 CLIP = 90.0
 WIDE = 256
 HOP = 128
+ROWS = 32
 F32 = jnp.float32
 BF16 = jnp.bfloat16
 MESH = pl.DeviceIdType.MESH
@@ -62,7 +63,7 @@
     heads = dt_ref.shape[0]
     width = WIDE if channels % WIDE == 0 else HOP
     chunks = channels // width
-    hops = channels // HOP
+    hops = channels // HOP * (N // ROWS)
     seq = lax.axis_index("seq")
     ten = lax.axis_index("tensor")
     lin = lax.axis_index("section") * n_ten + ten
@@ -146,17 +147,19 @@
     bt[...] = b_ref[...].astype(F32).T.astype(BF16)
     ct[...] = c_ref[...].astype(F32).T.astype(BF16)
 
+    def piece_of(k):
+        per = N // ROWS
+        return pl.ds(pl.multiple_of(k % per * ROWS, ROWS), ROWS), pl.ds(pl.multiple_of(k // per * HOP, HOP), HOP)
+
     def forward_hop(k):
-        cols = pl.ds(pl.multiple_of(k * HOP, HOP), HOP)
         return pltpu.make_async_remote_copy(
-            src_ref=sout.at[:, cols], dst_ref=sin.at[:, cols], send_sem=fs.at[k], recv_sem=fr.at[k],
+            src_ref=sout.at[piece_of(k)], dst_ref=sin.at[piece_of(k)], send_sem=fs.at[k], recv_sem=fr.at[k],
             device_id=seq_peer((seq + 1) % n_seq), device_id_type=MESH,
         )
 
     def backward_hop(k):
-        cols = pl.ds(pl.multiple_of(k * HOP, HOP), HOP)
         return pltpu.make_async_remote_copy(
-            src_ref=gout.at[:, cols], dst_ref=gin.at[:, cols], send_sem=bs.at[k], recv_sem=br.at[k],
+            src_ref=gout.at[piece_of(k)], dst_ref=gin.at[piece_of(k)], send_sem=bs.at[k], recv_sem=br.at[k],
             device_id=seq_peer((seq + n_seq - 1) % n_seq), device_id_type=MESH,
         )
 
@@ -164,8 +167,8 @@
         return pex[tokens - 1 : tokens, cols]
 
     def hops_of(c):
-        per = width // HOP
-        return [(c * per + i, pl.ds(pl.multiple_of((c * per + i) * HOP, HOP), HOP)) for i in range(per)]
+        per = width // HOP * (N // ROWS)
+        return [(c * per + i, piece_of(c * per + i)) for i in range(per)]
 
     def first(c, cols):
         sel = picks(3 * heads, c).astype(BF16)
@@ -179,8 +182,8 @@
 
         @pl.when(seq == 0)
         def _():
-            for k, part in hops_of(c):
-                sout[:, part] = total_decay(part) * bx[:, part]
+            for k, (rows, part) in hops_of(c):
+                sout[rows, part] = total_decay(part) * bx[rows, part]
                 forward_hop(k).start()
 
     load_values.wait()
@@ -222,12 +225,12 @@
     def third(c, cols):
         @pl.when(seq > 0)
         def _():
-            for k, part in hops_of(c):
+            for k, (rows, part) in hops_of(c):
                 forward_hop(k).wait_recv()
 
                 @pl.when(seq < n_seq - 1)
                 def _():
-                    sout[:, part] = total_decay(part) * (sin[:, part] + bx[:, part])
+                    sout[rows, part] = total_decay(part) * (sin[rows, part] + bx[rows, part])
                     forward_hop(k).start()
 
         hi, lo = split2(sin[:, cols])
@@ -269,8 +272,8 @@
 
         @pl.when(seq == n_seq - 1)
         def _():
-            for k, part in hops_of(c):
-                gout[:, part] = ce[:, part]
+            for k, (rows, part) in hops_of(c):
+                gout[rows, part] = ce[rows, part]
                 backward_hop(k).start()
 
     loop(fourth)
@@ -306,12 +309,12 @@
 
         @pl.when(seq < n_seq - 1)
         def _():
-            for k, part in hops_of(c):
+            for k, (rows, part) in hops_of(c):
                 backward_hop(k).wait_recv()
 
                 @pl.when(seq > 0)
                 def _():
-                    gout[:, part] = ce[:, part] + total_decay(part) * gin[:, part]
+                    gout[rows, part] = ce[rows, part] + total_decay(part) * gin[rows, part]
                     backward_hop(k).start()
 
         e_grad = total_decay(cols) * gin[:, cols]
@@ -353,13 +356,11 @@
 
     @pl.when(seq < n_seq - 1)
     def _():
-        for k in range(hops):
-            forward_hop(k).wait_send()
+        lax.fori_loop(0, hops, lambda k, carry: (forward_hop(k).wait_send(), carry)[1], 0)
 
     @pl.when(seq > 0)
     def _():
-        for k in range(hops):
-            backward_hop(k).wait_send()
+        lax.fori_loop(0, hops, lambda k, carry: (backward_hop(k).wait_send(), carry)[1], 0)
 
     wait_all(scb, lin, n_lin, lin_peer, sc_s, sc_r)
     total = total_of(scb, n_lin)
@@ -386,7 +387,7 @@
     n_lin = n_sec * n_ten
     tokens, channels = values.shape
     heads = decay_rate.shape[0]
-    hops = channels // HOP
+    hops = channels // HOP * (N // ROWS)
     shape = jax.ShapeDtypeStruct
     vm = pltpu.VMEM
     wide32 = vm((tokens, channels), F32)

time: 62.6 us -> 60.2 us (0.962)
  Pallas kernels: 61.8 us -> 59.3 us
    pallas_call x1, Pallas kernels: 59.4 us -> 56.9 us  [local(): pl.pallas_call(functools.partial(kernel, (n_sec, n_seq, n_ten)), out_shap...]
where the time goes in v3:
time: 60.2 us; the launch traced here: 59.9 us
  Pallas kernels  59.3 us (99%)
  between operations  0.64 us (1%)
    pallas_call x1, Pallas kernels, local(): pl.pallas_call(functools.partial(kernel, (n_sec, n_seq, n_ten)), out_shap...  56.9 us
    pallas_call x1, Pallas kernels, local(): pl.pallas_call(write_out, out_shape=tuple((shape(x.shape, x.dtype) for x...  2.41 us

profile of v3, /device:TPU:0, one launch (start us, length us, event | category | flops | bytes accessed | tf_op | source)
XLA Modules:
  0.0 59.9 jit_solution(3588385460127748094)
XLA Ops:
  0.6 56.9 %shard_map.143 = (bf16[256,1024]{1,0:T(8,128)(2,1)}, bf16[256,1024]{1,0:T(8,128)(2,1)}, bf16[256,1024]{1,0:T(8,128)(2,1)}, f32[256,128]{1,0:T(8,128)}, f32[256,1...) custom-call(bf16[256,1024]{1,0:T(8,128)(2,1)} %v_in.1, bf16[256,1024]{1,0:T(8,128)(2,1)} %g_in.1, ...), custom_call_target="tpu_custom_call" | custom-call | tf_op jit(solution)/shard_map/pallas_call | solution.py:399
  57.5 2.4 %shard_map.144 = (bf16[256,1024]{1,0:T(8,128)(2,1)}, bf16[256,1024]{1,0:T(8,128)(2,1)}, bf16[256,1024]{1,0:T(8,128)(2,1)}, f32[256,128]{1,0:T(8,128)}, f32[256,1...) custom-call(bf16[256,1024]{1,0:T(8,128)(2,1)} %get-tuple-element.24.refs_0_, ...), custom_call_target="tpu_custom_call" | custom-call | tf_op jit(solution)/shard_map/pallas_call | solution.py:433

commit v4 on v3

--- a/solution.py
+++ b/solution.py
@@ -207,7 +207,20 @@
     mt_hi[...] = hi
     mt_lo[...] = lo
 
+    def forward_relay(c):
+        for k, (rows, part) in hops_of(c):
+            forward_hop(k).wait_recv()
+
+            @pl.when(seq < n_seq - 1)
+            def _():
+                sout[rows, part] = total_decay(part) * (sin[rows, part] + bx[rows, part])
+                forward_hop(k).start()
+
     def second(c, cols):
+        @pl.when((seq > 0) & (2 * seq < n_seq))
+        def _():
+            forward_relay(c)
+
         gate = g_ref[:, cols].astype(F32)
         sigm = 1.0 / (1.0 + jnp.exp(-gate))
         swi[:, cols] = gate * sigm
@@ -223,15 +236,9 @@
     inn[...] = jnp.zeros_like(inn)
 
     def third(c, cols):
-        @pl.when(seq > 0)
+        @pl.when(2 * seq >= n_seq)
         def _():
-            for k, (rows, part) in hops_of(c):
-                forward_hop(k).wait_recv()
-
-                @pl.when(seq < n_seq - 1)
-                def _():
-                    sout[rows, part] = total_decay(part) * (sin[rows, part] + bx[rows, part])
-                    forward_hop(k).start()
+            forward_relay(c)
 
         hi, lo = split2(sin[:, cols])
         mixed = pex[:, cols] * (mix[:, cols] + (nn(c_ref[...], hi) + nn(c_ref[...], lo)))

time: 60.2 us -> 60.2 us (level)
  no operation moved by 1% of the time
where the time goes in v4:
time: 60.2 us; the launch traced here: 60 us
  Pallas kernels  59.3 us (99%)
  between operations  0.64 us (1%)
    pallas_call x1, Pallas kernels, local(): pl.pallas_call(functools.partial(kernel, (n_sec, n_seq, n_ten)), out_shap...  56.9 us
    pallas_call x1, Pallas kernels, local(): pl.pallas_call(write_out, out_shape=tuple((shape(x.shape, x.dtype) for x...  2.41 us

profile of v4, /device:TPU:0, one launch (start us, length us, event | category | flops | bytes accessed | tf_op | source)
XLA Modules:
  0.0 60.0 jit_solution(7049441307931163506)
XLA Ops:
  0.6 56.9 %shard_map.143 = (bf16[256,1024]{1,0:T(8,128)(2,1)}, bf16[256,1024]{1,0:T(8,128)(2,1)}, bf16[256,1024]{1,0:T(8,128)(2,1)}, f32[256,128]{1,0:T(8,128)}, f32[256,1...) custom-call(bf16[256,1024]{1,0:T(8,128)(2,1)} %v_in.1, bf16[256,1024]{1,0:T(8,128)(2,1)} %g_in.1, ...), custom_call_target="tpu_custom_call" | custom-call | tf_op jit(solution)/shard_map/pallas_call | solution.py:406
  57.6 2.4 %shard_map.144 = (bf16[256,1024]{1,0:T(8,128)(2,1)}, bf16[256,1024]{1,0:T(8,128)(2,1)}, bf16[256,1024]{1,0:T(8,128)(2,1)}, f32[256,128]{1,0:T(8,128)}, f32[256,1...) custom-call(bf16[256,1024]{1,0:T(8,128)(2,1)} %get-tuple-element.24.refs_0_, ...), custom_call_target="tpu_custom_call" | custom-call | tf_op jit(solution)/shard_map/pallas_call | solution.py:440
